TPU v7x, 32 devices: a whole 2x2x4 slice. The times are simulated.
32 devices in a mesh: group: 1, ep: 32 (over z, y, x, core), sub: 1.
Axes of the slice: x: 2, y: 2, z: 4, core: 2. Of those that a mesh axis runs over, the one named last changes fastest.
Arguments:
- hidden: bfloat16 [256, 4096], P(('group', 'ep', 'sub')), may hold values from -6 to 6
- query: bfloat16 [256, 4096], P(('group', 'ep', 'sub')), may hold values from -120 to 120
- cached_key_store: bfloat16 [256, 32, 256], P(('group', 'ep', 'sub')), may hold values from -4.5 to 4.5
- cached_value_store: bfloat16 [256, 32, 256], P(('group', 'ep', 'sub')), may hold values from -9 to 9
- current_key: bfloat16 [256, 256], P(('group', 'ep', 'sub')), may hold values from -6 to 6
- current_value: bfloat16 [256, 256], P(('group', 'ep', 'sub')), may hold values from -9 to 9
- norm_gain: float32 [4096], replicated, may hold values from 0.1 to 1.9
- expert_ids: int32 [256, 8], P(('group', 'ep')), may hold values from 0 to 15, all different within a row; in each aligned block of 8 rows (0 to 7, 8 to 15, ...) at most 4 rows name the same one
- gate_weights: float32 [256, 8], P(('group', 'ep')), may hold values from 0.05 to 0.35
- w_gate: bfloat16 [32, 4096, 384], P('ep', None, 'sub'), may hold values from -0.09375 to 0.09375
- w_up: bfloat16 [32, 4096, 384], P('ep', None, 'sub'), may hold values from -0.09375 to 0.09375
- w_down: bfloat16 [32, 384, 4096], P('ep', None, 'sub'), may hold values from -0.21875 to 0.21875
Outputs:
- ffn_out: bfloat16 [256, 4096], P(('group', 'ep'), 'sub')
Inputs may be any that keep to these rules, and one draw needn't show every extreme that they name: `expert_ids`: each token names 8 different experts; within the rows of one device (aligned blocks of 8 rows) no expert is named by more than 4 rows, a bound that some block reaches.
All inputs are finite; a program needn't handle non-finite values.
Results may differ from a plain program's by a relative error of at most 0.019.
Values may be sent and summed in bfloat16 or wider, within the bound.
A program may use at most 64 MiB of HBM per device.

v0:
```python
import math

import jax
import jax.numpy as jnp
from jax import lax
from jax.sharding import PartitionSpec as P

QUERY_HEADS = 32
KEY_VALUE_HEADS = 2
HEAD_SIZE = 128
FF = 768


epsilon = 1e-06


def attend_norm(
    hidden, query, cached_key_store, cached_value_store, current_key, current_value, norm_gain
):
    count_of_rows = hidden.shape[0]
    context_output = cached_key_store.shape[1]
    query_group_width = QUERY_HEADS // KEY_VALUE_HEADS
    scaling = 1.0 / math.sqrt(HEAD_SIZE)
    query_rows = query.reshape(count_of_rows, KEY_VALUE_HEADS, query_group_width, HEAD_SIZE)
    key_row_block = cached_key_store.reshape(
        count_of_rows, context_output, KEY_VALUE_HEADS, HEAD_SIZE
    )
    value_row_block = cached_value_store.reshape(
        count_of_rows, context_output, KEY_VALUE_HEADS, HEAD_SIZE
    )
    incoming_key = current_key.reshape(count_of_rows, KEY_VALUE_HEADS, HEAD_SIZE)
    incoming_value = current_value.reshape(count_of_rows, KEY_VALUE_HEADS, HEAD_SIZE)
    old_scores = (
        jnp.einsum("tgqd,tpgd->tgqp", query_rows, key_row_block, preferred_element_type=jnp.float32)
        * scaling
    )
    new_scores = (
        jnp.einsum("tgqd,tgd->tgq", query_rows, incoming_key, preferred_element_type=jnp.float32)
        * scaling
    )
    top_score = jnp.maximum(jnp.max(old_scores, axis=-1), new_scores)
    old_exp = jnp.exp(old_scores - top_score[..., None])
    new_exp = jnp.exp(new_scores - top_score)
    denominator = jnp.sum(old_exp, axis=-1) + new_exp
    old_probs = (old_exp / denominator[..., None]).astype(jnp.bfloat16)
    new_probs = (new_exp / denominator).astype(jnp.bfloat16)
    attended = jnp.einsum(
        "tgqp,tpgd->tgqd", old_probs, value_row_block, preferred_element_type=jnp.float32
    )
    attended = (
        attended
        + new_probs.astype(jnp.float32)[..., None]
        * incoming_value.astype(jnp.float32)[:, :, None, :]
    )
    resid = hidden.astype(jnp.float32) + attended.reshape(count_of_rows, QUERY_HEADS * HEAD_SIZE)
    meansq = jnp.mean(resid * resid, axis=-1, keepdims=True)
    return (resid * lax.rsqrt(meansq + epsilon) * norm_gain).astype(jnp.bfloat16)


def slot_targets(chosen, experts, capacity):
    flattened = chosen.reshape(-1)
    onehot = (flattened[:, None] == jnp.arange(experts, dtype=jnp.int32)[None, :]).astype(jnp.int32)
    slot_rank = jnp.sum((jnp.cumsum(onehot, axis=0) - onehot) * onehot, axis=1)
    return (flattened * capacity + slot_rank).reshape(chosen.shape)


def pack_rows(normed, target, experts, capacity, spread):
    model_width = normed.shape[1]
    all_slots = jnp.arange(experts * capacity, dtype=jnp.int32)
    match = all_slots[:, None, None] == target[None, :, :]
    picker = jnp.any(match, axis=2).astype(jnp.bfloat16)
    packed = jnp.dot(picker, normed, preferred_element_type=jnp.float32).astype(jnp.bfloat16)
    packed = packed.reshape(experts, 1, capacity, model_width)
    widened = jnp.broadcast_to(packed, (experts, spread, capacity, model_width))
    return widened.reshape(experts * spread, capacity, model_width)


def expert_hidden(slot_rows, w_gate, w_up):
    flattened = slot_rows.reshape(-1, slot_rows.shape[-1])
    gated = jnp.dot(flattened, w_gate[0], preferred_element_type=jnp.float32)
    raised = jnp.dot(flattened, w_up[0], preferred_element_type=jnp.float32)
    activated = (jax.nn.silu(gated) * raised).astype(jnp.bfloat16)
    return activated.reshape(slot_rows.shape[:-1] + (activated.shape[1],))


def expert_down(activated, w_down):
    out_width = w_down.shape[2]
    portion = lax.all_gather(activated, "sub", axis=3, tiled=True)
    unit_rows = portion.reshape(-1, portion.shape[-1])
    unit_weights = w_down[0]
    running = jnp.dot(unit_rows, unit_weights, preferred_element_type=jnp.float32)
    return running.astype(jnp.bfloat16).reshape(activated.shape[:3] + (out_width,))


def moe_block(
    normed, ids_pair, gates_pair, w_gate, w_up, w_down, experts, spread, capacity, sub_place
):
    pair_count = ids_pair.shape[0]
    count_of_rows = ids_pair.shape[1]
    targets = jnp.stack(
        [slot_targets(ids_pair[side], experts, capacity) for side in range(pair_count)]
    )
    own_targets = lax.dynamic_index_in_dim(targets, sub_place, 0, keepdims=False)
    outgoing = pack_rows(normed, own_targets, experts, capacity, spread)
    arrived = lax.all_to_all(outgoing, "ep", split_axis=0, concat_axis=0, tiled=True)
    activated = expert_hidden(
        lax.all_gather(arrived[None], "sub", axis=0, tiled=True), w_gate, w_up
    )
    partial_rows = expert_down(activated, w_down)
    returned = lax.all_to_all(partial_rows, "ep", split_axis=1, concat_axis=1, tiled=True)
    shaped = returned.reshape(pair_count, experts, spread, capacity, returned.shape[3])
    summed = jnp.sum(shaped, axis=2, dtype=jnp.float32)
    contract = "snec,sech->snh"
    columns = jnp.arange(experts * capacity, dtype=jnp.int32)
    selected = (targets[..., None] == columns).astype(jnp.float32)
    mixing = jnp.einsum("snk,snkc->snc", gates_pair, selected, precision=lax.Precision.HIGHEST)
    mixing = mixing.reshape(pair_count, count_of_rows, experts, capacity)
    return jnp.einsum(contract, mixing, summed, precision=lax.Precision.HIGHEST).astype(
        jnp.bfloat16
    )


def shards(
    hidden,
    query,
    cached_key_store,
    cached_value_store,
    current_key,
    current_value,
    norm_gain,
    expert_ids,
    gate_weights,
    w_gate,
    w_up,
    w_down,
):
    ep_count = lax.axis_size("ep")
    sub_count = lax.axis_size("sub")
    sub_place = lax.axis_index("sub")
    count_of_rows = hidden.shape[0]
    chosen_count = expert_ids.shape[1]
    slice_units = sub_count * w_gate.shape[2]
    spread = FF // slice_units
    experts = ep_count // spread
    capacity = max(2, count_of_rows * chosen_count // experts)
    ids_pair = expert_ids.reshape(sub_count, count_of_rows, chosen_count)
    gates_pair = gate_weights.reshape(sub_count, count_of_rows, chosen_count)
    normed = attend_norm(
        hidden, query, cached_key_store, cached_value_store, current_key, current_value, norm_gain
    )
    merged = moe_block(
        normed, ids_pair, gates_pair, w_gate, w_up, w_down, experts, spread, capacity, sub_place
    )
    return merged.reshape(sub_count * count_of_rows, merged.shape[2])


def solution(mesh):
    return jax.shard_map(
        shards,
        mesh=mesh,
        in_specs=(
            P(("group", "ep", "sub"), None),
            P(("group", "ep", "sub"), None),
            P(("group", "ep", "sub"), None, None),
            P(("group", "ep", "sub"), None, None),
            P(("group", "ep", "sub"), None),
            P(("group", "ep", "sub"), None),
            P(),
            P(("group", "ep"), None),
            P(("group", "ep"), None),
            P("ep", None, "sub"),
            P("ep", None, "sub"),
            P("ep", None, "sub"),
        ),
        out_specs=P(("group", "ep"), "sub"),
        check_vma=False,
    )
```

profile of v0, /device:TPU:0, one launch (start us, length us, event | category | flops | bytes accessed | tf_op | source)
XLA Modules:
  0.0 92.4 jit_solution(9955598061423871379)
XLA Ops:
  0.0 0.0 copy-start
  0.0 1.4 %fusion.42 = (f32[8,2,16]{2,1,0:T(2,128)S(1)}, f32[8,2,16,32]{3,2,1,0:T(8,128)S(1)}) fusion(bf16[8,2,16,128]{3,0,2,1:T(8,128)(2,1)} %bitcast.72, bf16[8,32,256]{2,1,0:T(8,128)(2,1)} %param.14), kind=kOutput, calls=%fused_computation.57 | convolution fusion | flops 2113280 | bytes 230400 | tf_op jit(solution)/shard_map/tgqd,tpgd->tgqp/dot_general | solution.py:34
  1.4 1.0 %fusion.30 = f32[8,2,1,16]{3,2,1,0:T(1,128)S(1)} fusion(bf16[8,2,16,128]{3,0,2,1:T(8,128)(2,1)} %bitcast.73, bf16[8,2,128,1]{2,0,1,3:T(8,128)(2,1)} %bitcast.76), kind=kOutput, calls=%fused_computation.35 | convolution fusion | flops 65536 | bytes 70656 | tf_op jit(solution)/shard_map/tgqd,tgd->tgq/dot_general | solution.py:38
  2.4 0.2 fusion.24
  2.6 0.7 bitcast_convert_fusion
  3.3 1.2 %convolution_add_fusion = f32[8,2,16,128]{3,2,1,0:T(8,128)S(1)} fusion(f32[8,2,16,32]{3,2,1,0:T(8,128)S(1)} %get-tuple-element.8, f32[8,2,128]{2,1,0:T(2,128)S(1)} %copy.32, f32[8,2,16]{2,1,0:T(2,128)S(1)} %get-tuple-element.6, f32[8,2,16]{2,1,0:T(2,128)S(1)} %get-tuple-element.5, f32[8,2,16]{2,1,0:T(2,128)S(1)} %multiply_maximum_fusion, ...), kind=kOutput, calls=%fused_computation.12 | convolution fusion | flops 2187264 | bytes 306176 | tf_op jit(solution)/shard_map/tgqp,tpgd->tgqd/dot_general | solution.py:47
  4.5 1.0 %multiply_reduce_fusion = f32[8]{0:T(128)S(1)} fusion(f32[1,8,32,128]{3,2,1,0:T(8,128)S(1)} %bitcast.69, bf16[8,4096]{1,0:T(8,128)(2,1)} %param.12), kind=kLoop, calls=%fused_computation.26 | loop fusion | flops 131064 | bytes 196640 | tf_op jit(solution)/shard_map/reduce_sum | solution.py:56
  5.5 0.8 eq.44
  6.3 0.1 fusion.34
  6.4 0.1 reduce_window_sum.11
  6.5 0.2 select_reduce_fusion
  6.7 0.1 reduce_sum.39
  6.7 0.7 multiply_add_fusion
  7.4 0.1 fusion.35
  7.5 2.0 %convolution_convert_fusion.1 = bf16[64,4096]{1,0:T(8,128)(2,1)} fusion(pred[64,8]{0,1:T(8,128)(4,1)S(1)} %fusion.35, f32[1,8,32,128]{3,2,1,0:T(8,128)S(1)} %bitcast.70, bf16[8,4096]{1,0:T(8,128)(2,1)} %param.12, f32[4096]{0:T(1024)} %param.18, f32[8]{0:T(128)S(1)} %add_rsqrt_fusion), kind=kOutput, calls=%fused_computation.1 | convolution fusion | flops 4620288 | bytes 737824 | tf_op jit(solution)/shard_map/dot_general | solution.py:72
  9.5 2.0 %broadcast_in_dim.4 = bf16[16,4,4096]{2,1,0:T(4,128)(2,1)} reshape(bf16[64,4096]{1,0:T(8,128)(2,1)} %convolution_convert_fusion.1) | data formatting | bytes 1048576 | tf_op jit(solution)/shard_map/broadcast_in_dim | solution.py:74
  11.6 1.5 %broadcast_in_dim.5 = bf16[16,2,4,4096]{3,2,1,0:T(4,128)(2,1)S(1)} broadcast(bf16[16,4,4096]{2,1,0:T(4,128)(2,1)} %broadcast_in_dim.4), dimensions={0,2,3} | broadcast | bytes 1572864 | tf_op jit(solution)/shard_map/broadcast_in_dim | solution.py:74
  13.1 33.4 %all_to_all.10 = bf16[32,4,4096]{2,1,0:T(4,128)(2,1)} all-to-all(bf16[32,4,4096]{2,1,0:T(4,128)(2,1)S(1)} %bitcast.68), channel_id=1, replica_groups=mesh['group'=1,'ep'=32,'sub'=1] {'ep'}, dimensions={0} | all-to-all | bytes 2097152 | tf_op jit(solution)/shard_map/all_to_all | solution.py:105
  46.6 2.2 %reshape.108 = bf16[128,4096]{1,0:T(8,128)(2,1)} reshape(bf16[32,4,4096]{2,1,0:T(4,128)(2,1)} %all_to_all.10) | data formatting | bytes 2097152 | tf_op jit(solution)/shard_map/reshape | solution.py:79
  48.7 2.9 %fusion.4 = f32[128,384]{1,0:T(8,128)S(1)} fusion(bf16[128,4096]{1,0:T(8,128)(2,1)} %reshape.108, bf16[1,4096,384]{2,1,0:T(8,128)(2,1)} %param.21), kind=kOutput, calls=%fused_computation.7 | convolution fusion | flops 402653184 | bytes 4390912 | tf_op jit(solution)/shard_map/dot_general | solution.py:80
  51.6 0.0 copy-done
  51.7 4.6 %convolution_convert_fusion = bf16[128,4096]{1,0:T(8,128)(2,1)} fusion(bf16[1,384,4096]{2,1,0:T(8,128)(2,1)S(1)} %copy-done, bf16[128,4096]{1,0:T(8,128)(2,1)} %reshape.108, bf16[1,4096,384]{2,1,0:T(8,128)(2,1)} %param.22, f32[128,384]{1,0:T(8,128)S(1)} %fusion.4), kind=kOutput, calls=%fused_computation | convolution fusion | flops 806125568 | bytes 8585216 | tf_op jit(solution)/shard_map/dot_general | solution.py:91
  56.3 0.0 copy-start.1
  56.3 2.3 %reshape.109 = bf16[1,32,4,4096]{3,2,1,0:T(4,128)(2,1)} reshape(bf16[128,4096]{1,0:T(8,128)(2,1)} %convolution_convert_fusion) | data formatting | bytes 2097152 | tf_op jit(solution)/shard_map/reshape | solution.py:92
  58.6 3.7 %all-to-all-start.1 = ((bf16[1,32,4,4096]{3,2,0,1:T(4,128)(2,1)}), bf16[1,32,4,4096]{3,2,0,1:T(4,128)(2,1)}, u32[]{:S(2)}, u32[]{:S(2)}) async-start(bf16[1,32,4,4096]{3,2,0,1:T(4,128)(2,1)} %bitcast.67), calls=%async_computation.1 | async-start | bytes 2097152 | tf_op jit(solution)/shard_map/all_to_all | solution.py:110
  62.3 0.0 copy-done.1
  62.3 0.2 fusion.36
  62.5 0.1 copy.37
  62.6 25.9 %all-to-all-done.1 = bf16[1,32,4,4096]{3,2,0,1:T(4,128)(2,1)} async-done(((bf16[1,32,4,4096]{3,2,0,1:T(4,128)(2,1)}), bf16[1,32,4,4096]{3,2,0,1:T(4,128)(2,1)}, u32[]{:S(2)}, u32[]{:S(2)}) %all-to-all-start.1) | async-done | bytes 1048608 | tf_op jit(solution)/shard_map/all_to_all | solution.py:110
  88.5 2.1 %convert_reduce_fusion = f32[16,4,4096]{2,1,0:T(4,128)S(1)} fusion(bf16[16,2,4,4096]{3,2,1,0:T(4,128)(2,1)} %bitcast.21), kind=kLoop, calls=%fused_computation.9 | loop fusion | flops 786432 | bytes 2097152 | tf_op jit(solution)/shard_map/reduce_sum | solution.py:112
  90.6 1.8 %fusion = bf16[8,4096]{1,0:T(8,128)(2,1)} fusion(f32[16,4,4096]{2,1,0:T(4,128)S(1)} %convert_reduce_fusion, f32[8,16,4]{0,2,1:T(4,128)S(1)} %bitcast.71), kind=kOutput, calls=%fused_computation.3 | convolution fusion | flops 25198592 | bytes 1116160 | tf_op jit(solution)/shard_map/snec,sech->snh/dot_general | solution.py:118
  (4 shorter events, 0.1 us)
Async XLA Ops:
  0.0 51.6 %copy-start = (bf16[1,384,4096]{2,1,0:T(8,128)(2,1)S(1)}, bf16[1,384,4096]{2,1,0:T(8,128)(2,1)}, u32[]{:S(2)}) copy-start(bf16[1,384,4096]{2,1,0:T(8,128)(2,1)} %param.23) | copy-start | bytes 9437188
  56.3 6.0 %copy-start.1 = (f32[8,8]{1,0:T(8,128)S(1)}, f32[8,8]{1,0:T(8,128)}, u32[]{:S(2)}) copy-start(f32[8,8]{1,0:T(8,128)} %param.20) | copy-start | bytes 772
  58.6 30.0 %all-to-all-start.1 = ((bf16[1,32,4,4096]{3,2,0,1:T(4,128)(2,1)}), bf16[1,32,4,4096]{3,2,0,1:T(4,128)(2,1)}, u32[]{:S(2)}, u32[]{:S(2)}) async-start(bf16[1,32,4,4096]{3,2,0,1:T(4,128)(2,1)} %bitcast.67), calls=%async_computation.1 | async-start | bytes 2097152 | tf_op jit(solution)/shard_map/all_to_all | solution.py:110
where the time goes:
time: 93.1 us; the launch traced here: 92.4 us
  blocking collectives  33.4 us (36%)
  waiting for transfers between devices  25.9 us (28%)
  matrix products  15.1 us (16%)
  local copies, waits for them, and re-layouts  8.94 us (10%)
  other arithmetic  5.24 us (6%)
  starting transfers between devices  3.75 us (4%)
    all_to_all x1, blocking collectives, moe_block(): lax.all_to_all(outgoing, 'ep', split_axis=0, concat_axis=0, tiled=True)  33.4 us
    all_to_all x1, waiting for transfers between devices, moe_block(): lax.all_to_all(partial_rows, 'ep', split_axis=1, concat_axis=1, tiled=True)  25.9 us
    dot_general x1, matrix products, expert_down(): jnp.dot(unit_rows, unit_weights, preferred_element_type=jnp.float32)  4.63 us
    all_to_all x1, starting transfers between devices, moe_block(): lax.all_to_all(partial_rows, 'ep', split_axis=1, concat_axis=1, tiled=True)  3.75 us
    broadcast_in_dim x2, local copies, waits for them, and re-layouts, pack_rows(): widened = jnp.broadcast_to(packed, (experts, spread, capacity, model_width))  3.57 us
    dot_general x1, matrix products, expert_hidden(): gated = jnp.dot(flattened, w_gate[0], preferred_element_type=jnp.float32)  2.92 us
    reshape x1, local copies, waits for them, and re-layouts, expert_down(): running.astype(jnp.bfloat16).reshape(activated.shape[:3] + (out_width,))  2.27 us
    reshape x1, local copies, waits for them, and re-layouts, expert_hidden(): flattened = slot_rows.reshape(-1, slot_rows.shape[-1])  2.15 us
  transfers between devices with their start and end apart: 1, of which 1 were waited for; matrix products, arithmetic and copies ran while one was open for 0% of the time, Pallas kernels for 0%

commit v1 on v0

--- a/solution.py
+++ b/solution.py
@@ -1,8 +1,11 @@
+import functools
 import math
 
 import jax
 import jax.numpy as jnp
 from jax import lax
+from jax.experimental import pallas as pl
+from jax.experimental.pallas import tpu as pltpu
 from jax.sharding import PartitionSpec as P
 
 QUERY_HEADS = 32
@@ -118,6 +121,391 @@
     return jnp.einsum(contract, mixing, summed, precision=lax.Precision.HIGHEST).astype(
         jnp.bfloat16
     )
+
+
+CAPACITY = 4
+ROWS = 8
+BLOCK = 16
+PARTS = 2
+F32 = jnp.float32
+BF16 = jnp.bfloat16
+
+
+def attention_rows(hidden_ref, query_ref, keys_ref, values_ref, new_key_ref, new_value_ref, gain_ref):
+    positions = keys_ref.shape[1]
+    group = QUERY_HEADS // KEY_VALUE_HEADS
+    scaling = 1.0 / math.sqrt(HEAD_SIZE)
+    query = query_ref[...].astype(F32)
+    rows, columns = group * ROWS, ROWS * positions
+    row_token = lax.broadcasted_iota(jnp.int32, (rows, columns), 0) % ROWS
+    column_token = lax.broadcasted_iota(jnp.int32, (rows, columns), 1) // positions
+    own = row_token == column_token
+    pieces = []
+    for g in range(KEY_VALUE_HEADS):
+        lanes = slice(g * HEAD_SIZE, (g + 1) * HEAD_SIZE)
+        stacked = jnp.concatenate(
+            [
+                query[:, (g * group + h) * HEAD_SIZE : (g * group + h + 1) * HEAD_SIZE]
+                for h in range(group)
+            ],
+            axis=0,
+        )
+        keys = keys_ref[:, :, lanes].reshape(columns, HEAD_SIZE)
+        values = values_ref[:, :, lanes].reshape(columns, HEAD_SIZE)
+        scores = lax.dot_general(
+            stacked.astype(BF16), keys, (((1,), (1,)), ((), ())), preferred_element_type=F32
+        )
+        scores = jnp.where(own, scores * scaling, -1e30)
+        new_key = jnp.concatenate([new_key_ref[:, lanes].astype(F32)] * group, axis=0)
+        new_value = jnp.concatenate([new_value_ref[:, lanes].astype(F32)] * group, axis=0)
+        new_score = jnp.sum(stacked * new_key, axis=1, keepdims=True) * scaling
+        top = jnp.maximum(jnp.max(scores, axis=1, keepdims=True), new_score)
+        weights = jnp.exp(scores - top)
+        new_weight = jnp.exp(new_score - top)
+        total = jnp.sum(weights, axis=1, keepdims=True) + new_weight
+        probs = (weights / total).astype(BF16)
+        new_prob = (new_weight / total).astype(BF16).astype(F32)
+        attended = jnp.dot(probs, values, preferred_element_type=F32) + new_prob * new_value
+        pieces += [attended[h * ROWS : (h + 1) * ROWS] for h in range(group)]
+    resid = hidden_ref[...].astype(F32) + jnp.concatenate(pieces, axis=1)
+    meansq = jnp.mean(resid * resid, axis=1, keepdims=True)
+    return resid * lax.rsqrt(meansq + epsilon) * gain_ref[...]
+
+
+def slot_weights(ids_ref, gates_ref, chips, my_chip):
+    slots = chips * BLOCK
+    place = lax.broadcasted_iota(jnp.int32, (ROWS, slots), 1)
+    token = lax.broadcasted_iota(jnp.int32, (ROWS, slots), 0)
+    expert = (place // BLOCK + my_chip) % chips
+    quarter = 2 * ((place // 8) % 2) + ((place // 4) % 2 + (place // BLOCK) % 2) % 2
+    chosen = jnp.zeros((ROWS, slots), F32)
+    weight = jnp.zeros((ROWS, slots), F32)
+    for k in range(ids_ref.shape[1]):
+        hit = ids_ref[:, k : k + 1] == expert
+        chosen = jnp.where(hit, 1.0, chosen)
+        weight = jnp.where(hit, gates_ref[:, k : k + 1], weight)
+    rank = jnp.zeros((ROWS, slots), F32)
+    for t in range(ROWS - 1):
+        rank = rank + jnp.where(token > t, chosen[t : t + 1, :], 0.0)
+    live = jnp.where(rank == (place % CAPACITY).astype(F32), chosen, 0.0)
+    picker = jnp.concatenate([jnp.where(quarter == q, live, 0.0) for q in range(4)], axis=0)
+    mixing = jnp.concatenate(
+        [jnp.where(quarter == q, live * weight, 0.0) for q in range(4)], axis=0
+    )
+    return picker, mixing
+
+
+def layer_kernel(
+    chips,
+    hidden_ref,
+    query_ref,
+    keys_ref,
+    values_ref,
+    new_key_ref,
+    new_value_ref,
+    gain_ref,
+    ids_ref,
+    gates_ref,
+    gate_hbm,
+    up_hbm,
+    down_hbm,
+    out_ref,
+    gate,
+    up,
+    down,
+    outgoing,
+    arrived,
+    row_buffer,
+    gated,
+    raised,
+    activated,
+    mine,
+    give,
+    take,
+    replies,
+    answers,
+    mixed,
+    weight_sem,
+    send_sem,
+    recv_sem,
+    pass_send,
+    pass_recv,
+    swap_send,
+    swap_recv,
+    reply_send,
+    reply_recv,
+):
+    width = hidden_ref.shape[1]
+    part = width // PARTS
+    quarter = part // 4
+    plane_rows = chips * CAPACITY
+    me = lax.axis_index("ep")
+    my_chip, core = me // 2, me % 2
+    sibling = my_chip * 2 + (1 - core)
+
+    weight_copies = [
+        pltpu.make_async_copy(source.at[0], target, weight_sem.at[i])
+        for i, (source, target) in enumerate(((gate_hbm, gate), (up_hbm, up), (down_hbm, down)))
+    ]
+    for copy in weight_copies:
+        copy.start()
+
+    def peer(offset):
+        return {"ep": ((my_chip + offset) % chips) * 2 + core}
+
+    barrier = pltpu.get_barrier_semaphore()
+
+    def greet(k, carry):
+        pl.semaphore_signal(barrier, inc=1, device_id=peer(k), device_id_type=pl.DeviceIdType.MESH)
+        return carry
+
+    lax.fori_loop(1, chips, greet, 0)
+    pl.semaphore_signal(
+        barrier, inc=1, device_id={"ep": sibling}, device_id_type=pl.DeviceIdType.MESH
+    )
+
+    normed = attention_rows(
+        hidden_ref, query_ref, keys_ref, values_ref, new_key_ref, new_value_ref, gain_ref
+    )
+    picker, mixing = slot_weights(ids_ref, gates_ref, chips, my_chip)
+    picker = picker.T.astype(BF16)
+    mixed[...] = mixing
+
+    def block(k):
+        return pl.ds(pl.multiple_of(k * BLOCK, BLOCK), BLOCK)
+
+    def dispatch(h, k):
+        return pltpu.make_async_remote_copy(
+            src_ref=outgoing.at[h, block(k)],
+            dst_ref=arrived.at[h, 0, block(k)],
+            send_sem=send_sem.at[h, k],
+            recv_sem=recv_sem.at[h, k],
+            device_id=peer(k),
+            device_id_type=pl.DeviceIdType.MESH,
+        )
+
+    def pass_on(h, k):
+        return pltpu.make_async_remote_copy(
+            src_ref=arrived.at[h, 0, block(k)],
+            dst_ref=arrived.at[h, 1, block(k)],
+            send_sem=pass_send.at[h, k],
+            recv_sem=pass_recv.at[h, k],
+            device_id={"ep": sibling},
+            device_id_type=pl.DeviceIdType.MESH,
+        )
+
+    def swap(h):
+        return pltpu.make_async_remote_copy(
+            src_ref=give.at[h],
+            dst_ref=take.at[h],
+            send_sem=swap_send.at[h],
+            recv_sem=swap_recv.at[h],
+            device_id={"ep": sibling},
+            device_id_type=pl.DeviceIdType.MESH,
+        )
+
+    def reply(h, k):
+        return pltpu.make_async_remote_copy(
+            src_ref=replies.at[h, block(k)],
+            dst_ref=answers.at[h, block(k)],
+            send_sem=reply_send.at[h, k],
+            recv_sem=reply_recv.at[h, k],
+            device_id=peer(chips - k),
+            device_id_type=pl.DeviceIdType.MESH,
+        )
+
+    def each(first, body):
+        def step(k, carry):
+            body(k)
+            return carry
+
+        lax.fori_loop(first, chips, step, 0)
+
+    for h in range(PARTS):
+        stacked = jnp.concatenate(
+            [normed[:, h * part + q * quarter : h * part + (q + 1) * quarter] for q in range(4)],
+            axis=0,
+        ).astype(BF16)
+        packed = jnp.dot(picker, stacked, preferred_element_type=F32).astype(BF16)
+        outgoing[h] = packed
+        arrived[h, 0, 0:BLOCK] = packed[0:BLOCK]
+        if h == 0:
+            pl.semaphore_wait(barrier, chips)
+        each(1, lambda k: dispatch(h, k).start())
+        pass_on(h, 0).start()
+
+    low = lax.broadcasted_iota(jnp.int32, (chips // 2, 8, quarter), 1) < 4
+
+    def swap_halves(x):
+        return pltpu.roll(x, 4, axis=1)
+
+    for h in range(PARTS):
+
+        def relay(k):
+            dispatch(h, k).wait_recv()
+            pass_on(h, k).start()
+
+        each(1, relay)
+        for plane in range(2):
+            if plane == 1:
+                each(0, lambda k: pass_on(h, k).wait_recv())
+            tiles = arrived[h, plane].astype(F32).reshape(chips // 2, 2, 2, 8, quarter)
+            for p in range(2):
+                a, b = tiles[:, 0, p], tiles[:, 1, p]
+                first = jnp.where(low, a, b)
+                second = swap_halves(jnp.where(low, b, a))
+                for q, x in ((2 * p, first), (2 * p + 1, second)):
+                    row_buffer[
+                        plane * plane_rows : (plane + 1) * plane_rows,
+                        h * part + q * quarter : h * part + (q + 1) * quarter,
+                    ] = x.reshape(plane_rows, quarter).astype(BF16)
+        if h == 0:
+            weight_copies[0].wait()
+            weight_copies[1].wait()
+        x = row_buffer[:, h * part : (h + 1) * part]
+        gate_part = jnp.dot(x, gate[h * part : (h + 1) * part, :], preferred_element_type=F32)
+        up_part = jnp.dot(x, up[h * part : (h + 1) * part, :], preferred_element_type=F32)
+        if h == 0:
+            gated[...] = gate_part
+            raised[...] = up_part
+        else:
+            gated[...] += gate_part
+            raised[...] += up_part
+
+    activated[...] = (jax.nn.silu(gated[...]) * raised[...]).astype(BF16)
+    weight_copies[2].wait()
+    for h in range(PARTS):
+        for q in range(4):
+            columns = slice(h * part + q * quarter, h * part + (q + 1) * quarter)
+            y = jnp.dot(activated[...], down[:, columns], preferred_element_type=F32)
+            mine[:, columns] = y[:plane_rows]
+            give[h, :, q * quarter : (q + 1) * quarter] = y[plane_rows:].astype(BF16)
+        swap(h).start()
+    for h in range(PARTS):
+        swap(h).wait_recv()
+        halves = []
+        for p in range(2):
+            y = []
+            for q in (2 * p, 2 * p + 1):
+                columns = slice(h * part + q * quarter, h * part + (q + 1) * quarter)
+                whole = mine[:, columns] + take[h, :, q * quarter : (q + 1) * quarter].astype(F32)
+                y.append(whole.reshape(chips // 2, 8, quarter))
+            turned = swap_halves(y[1])
+            halves.append((jnp.where(low, y[0], turned), jnp.where(low, turned, y[0])))
+        for m in range(chips // 2):
+            for side in range(2):
+                start = (2 * m + side) * BLOCK
+                replies[h, start : start + BLOCK] = jnp.concatenate(
+                    [halves[0][side][m], halves[1][side][m]], axis=0
+                ).astype(BF16)
+        answers[h, 0:BLOCK] = replies[h, 0:BLOCK]
+        each(1, lambda k: reply(h, k).start())
+
+    mixing = mixed[...]
+    high = mixing.astype(BF16)
+    rest = mixing - high.astype(F32)
+    middle = rest.astype(BF16)
+    last = (rest - middle.astype(F32)).astype(BF16)
+    for h in range(PARTS):
+        each(1, lambda k: reply(h, k).wait_recv())
+        got = answers[h]
+        total = jnp.dot(high, got, preferred_element_type=F32)
+        total = total + jnp.dot(middle, got, preferred_element_type=F32)
+        total = total + jnp.dot(last, got, preferred_element_type=F32)
+        for q in range(4):
+            columns = slice(h * part + q * quarter, h * part + (q + 1) * quarter)
+            out_ref[:, columns] = total[q * ROWS : (q + 1) * ROWS].astype(out_ref.dtype)
+
+    for h in range(PARTS):
+        each(1, lambda k: dispatch(h, k).wait_send())
+        each(0, lambda k: pass_on(h, k).wait_send())
+        swap(h).wait_send()
+        each(1, lambda k: reply(h, k).wait_send())
+
+
+def fused_layer(
+    hidden,
+    query,
+    cached_key_store,
+    cached_value_store,
+    current_key,
+    current_value,
+    norm_gain,
+    expert_ids,
+    gate_weights,
+    w_gate,
+    w_up,
+    w_down,
+):
+    chips = lax.axis_size("ep") // 2
+    width = hidden.shape[1]
+    part = width // PARTS
+    slots = chips * BLOCK
+    units = w_gate.shape[2]
+    pair_rows = 2 * chips * CAPACITY
+    dma = pltpu.SemaphoreType.DMA
+    vmem = pl.BlockSpec(memory_space=pltpu.VMEM)
+    hbm = pl.BlockSpec(memory_space=pl.ANY)
+    return pl.pallas_call(
+        functools.partial(layer_kernel, chips),
+        out_shape=jax.ShapeDtypeStruct(hidden.shape, BF16),
+        in_specs=[vmem] * 9 + [hbm] * 3,
+        out_specs=vmem,
+        scratch_shapes=[
+            pltpu.VMEM((width, units), BF16),
+            pltpu.VMEM((width, units), BF16),
+            pltpu.VMEM((units, width), BF16),
+            pltpu.VMEM((PARTS, slots, part // 4), BF16),
+            pltpu.VMEM((PARTS, 2, slots, part // 4), BF16),
+            pltpu.VMEM((pair_rows, width), BF16),
+            pltpu.VMEM((pair_rows, units), F32),
+            pltpu.VMEM((pair_rows, units), F32),
+            pltpu.VMEM((pair_rows, units), BF16),
+            pltpu.VMEM((pair_rows // 2, width), F32),
+            pltpu.VMEM((PARTS, pair_rows // 2, part), BF16),
+            pltpu.VMEM((PARTS, pair_rows // 2, part), BF16),
+            pltpu.VMEM((PARTS, slots, part // 4), BF16),
+            pltpu.VMEM((PARTS, slots, part // 4), BF16),
+            pltpu.VMEM((4 * ROWS, slots), F32),
+            dma((3,)),
+            dma((PARTS, chips)),
+            dma((PARTS, chips)),
+            dma((PARTS, chips)),
+            dma((PARTS, chips)),
+            dma((PARTS,)),
+            dma((PARTS,)),
+            dma((PARTS, chips)),
+            dma((PARTS, chips)),
+        ],
+        compiler_params=pltpu.CompilerParams(
+            collective_id=0, has_side_effects=True, vmem_limit_bytes=48 * 1024 * 1024
+        ),
+        cost_estimate=pl.CostEstimate(
+            flops=6 * pair_rows * width * units,
+            bytes_accessed=6 * width * units,
+            transcendentals=pair_rows * units,
+        ),
+    )(
+        hidden,
+        query,
+        cached_key_store,
+        cached_value_store,
+        current_key,
+        current_value,
+        norm_gain.reshape(1, width),
+        expert_ids,
+        gate_weights,
+        w_gate,
+        w_up,
+        w_down,
+    )
+
+
+def takes_fused_layer(row_count, chosen_count, units):
+    if lax.axis_size("sub") != 1 or lax.axis_size("group") != 1 or 2 * units != FF:
+        return False
+    chips = lax.axis_size("ep") // 2
+    return row_count == ROWS and chips * CAPACITY == row_count * chosen_count and chips % 2 == 0
 
 
 def shards(
@@ -138,6 +526,21 @@
     sub_count = lax.axis_size("sub")
     sub_place = lax.axis_index("sub")
     count_of_rows = hidden.shape[0]
+    if takes_fused_layer(hidden.shape[0], expert_ids.shape[1], w_gate.shape[2]):
+        return fused_layer(
+            hidden,
+            query,
+            cached_key_store,
+            cached_value_store,
+            current_key,
+            current_value,
+            norm_gain,
+            expert_ids,
+            gate_weights,
+            w_gate,
+            w_up,
+            w_down,
+        )
     chosen_count = expert_ids.shape[1]
     slice_units = sub_count * w_gate.shape[2]
     spread = FF // slice_units

time: 93.1 us -> 49.8 us (0.53)
  Pallas kernels: 0 us -> 39.8 us
  blocking collectives: 33.4 us -> 0 us
  waiting for transfers between devices: 25.9 us -> 0 us
  matrix products: 15.1 us -> 0 us
  other arithmetic: 5.24 us -> 0 us
  starting transfers between devices: 3.75 us -> 0 us
    pallas_call x0 -> x1, Pallas kernels: none -> 39.8 us  [fused_layer(): pl.pallas_call(functools.partial(layer_kernel, chips), out_shape=jax.Shap...]
    all_to_all x1 -> x0, blocking collectives: 33.4 us -> none  [moe_block(): lax.all_to_all(outgoing, 'ep', split_axis=0, concat_axis=0, tiled=True)]
    all_to_all x1 -> x0, waiting for transfers between devices: 25.9 us -> none  [moe_block(): lax.all_to_all(partial_rows, 'ep', split_axis=1, concat_axis=1, tiled=True)]
    dot_general x8 -> x0, matrix products: 15.1 us -> none  [the longest x1 4.63 us: expert_down(): jnp.dot(unit_rows, unit_weights, preferred_element_type=jnp.float32)]
    unnamed x4 -> x21, local copies, waits for them, and re-layouts: 0.01 us -> 9.47 us
    reshape x2 -> x0, local copies, waits for them, and re-layouts: 4.42 us -> none  [the longest x1 2.27 us: expert_down(): running.astype(jnp.bfloat16).reshape(activated.shape[:3] + (out_width,))]
    all_to_all x1 -> x0, starting transfers between devices: 3.75 us -> none  [moe_block(): lax.all_to_all(partial_rows, 'ep', split_axis=1, concat_axis=1, tiled=True)]
    broadcast_in_dim x2 -> x0, local copies, waits for them, and re-layouts: 3.57 us -> none  [pack_rows(): widened = jnp.broadcast_to(packed, (experts, spread, capacity, model_width))]
  transfers between devices with their start and end apart: 1 -> 0, of which waited for: 1 -> 0; matrix products, arithmetic and copies ran while one was open for 0% -> 0% of each run, Pallas kernels for 0% -> 0%
where the time goes in v1:
time: 49.8 us; the launch traced here: 49.3 us
  Pallas kernels  39.8 us (80%)
  local copies, waits for them, and re-layouts  9.47 us (19%)
    pallas_call x1, Pallas kernels, fused_layer(): pl.pallas_call(functools.partial(layer_kernel, chips), out_shape=jax.Shap...  39.8 us
    unnamed x21, local copies, waits for them, and re-layouts  9.47 us

profile of v1, /device:TPU:0, one launch (start us, length us, event | category | flops | bytes accessed | tf_op | source)
XLA Modules:
  0.0 49.3 jit_solution(18165886480363638089)
XLA Ops:
  0.0 0.0 copy-start
  0.0 1.9 %copy-done = bf16[1,4096,384]{2,1,0:T(8,128)(2,1)S(1)} copy-done((bf16[1,4096,384]{2,1,0:T(8,128)(2,1)S(1)}, bf16[1,4096,384]{2,1,0:T(8,128)(2,1)}, u32[]{:S(2)}) %copy-start) | copy-done | bytes 3145752
  1.9 0.0 copy-start.1
  1.9 0.9 %copy-done.1 = bf16[8,32,256]{2,1,0:T(8,128)(2,1)S(1)} copy-done((bf16[8,32,256]{2,1,0:T(8,128)(2,1)S(1)}, bf16[8,32,256]{2,1,0:T(8,128)(2,1)}, u32[]{:S(2)}) %copy-start.1) | copy-done | bytes 131096
  2.8 0.0 copy-start.2
  2.8 0.9 %copy-done.2 = bf16[8,32,256]{2,1,0:T(8,128)(2,1)S(1)} copy-done((bf16[8,32,256]{2,1,0:T(8,128)(2,1)S(1)}, bf16[8,32,256]{2,1,0:T(8,128)(2,1)}, u32[]{:S(2)}) %copy-start.2) | copy-done | bytes 131096
  3.7 0.0 copy-start.3
  3.7 0.8 %copy-done.3 = bf16[8,4096]{1,0:T(8,128)(2,1)S(1)} copy-done((bf16[8,4096]{1,0:T(8,128)(2,1)S(1)}, bf16[8,4096]{1,0:T(8,128)(2,1)}, u32[]{:S(2)}) %copy-start.3) | copy-done | bytes 65560
  4.5 0.0 copy-start.4
  4.5 0.8 %copy-done.4 = bf16[8,4096]{1,0:T(8,128)(2,1)S(1)} copy-done((bf16[8,4096]{1,0:T(8,128)(2,1)S(1)}, bf16[8,4096]{1,0:T(8,128)(2,1)}, u32[]{:S(2)}) %copy-start.4) | copy-done | bytes 65560
  5.4 0.0 copy-start.5
  5.4 0.7 %copy-done.5 = f32[4096]{0:T(1024)S(1)} copy-done((f32[4096]{0:T(1024)S(1)}, f32[4096]{0:T(1024)}, u32[]{:S(2)}) %copy-start.5) | copy-done | bytes 16408
  6.1 0.0 copy-start.6
  6.1 0.7 %copy-done.6 = bf16[8,256]{1,0:T(8,128)(2,1)S(1)} copy-done((bf16[8,256]{1,0:T(8,128)(2,1)S(1)}, bf16[8,256]{1,0:T(8,128)(2,1)}, u32[]{:S(2)}) %copy-start.6) | copy-done | bytes 4120
  6.8 0.0 copy-start.7
  6.8 0.7 %copy-done.7 = bf16[8,256]{1,0:T(8,128)(2,1)S(1)} copy-done((bf16[8,256]{1,0:T(8,128)(2,1)S(1)}, bf16[8,256]{1,0:T(8,128)(2,1)}, u32[]{:S(2)}) %copy-start.7) | copy-done | bytes 4120
  7.5 0.0 copy-start.8
  7.5 0.7 %copy-done.8 = s32[8,8]{1,0:T(8,128)S(1)} copy-done((s32[8,8]{1,0:T(8,128)S(1)}, s32[8,8]{1,0:T(8,128)}, u32[]{:S(2)}) %copy-start.8) | copy-done | bytes 280
  8.2 0.0 copy-start.9
  8.2 0.7 %copy-done.9 = f32[8,8]{1,0:T(8,128)S(1)} copy-done((f32[8,8]{1,0:T(8,128)S(1)}, f32[8,8]{1,0:T(8,128)}, u32[]{:S(2)}) %copy-start.9) | copy-done | bytes 280
  8.8 39.8 %shard_map.118 = bf16[8,4096]{1,0:T(8,128)(2,1)S(1)} custom-call(bf16[8,4096]{1,0:T(8,128)(2,1)S(1)} %copy-done.3, bf16[8,4096]{1,0:T(8,128)(2,1)S(1)} %copy-done.4, bf16[8,32,256]{2,1,0:T(8,128)(2,1)S(1)} %copy-done.1, bf16[8,32,256]{2,1,0:T(8,128)(2,1)S(1)} %copy-done.2, bf16[8,256]{1,0:T(8,128)(2,1)S(1)} %copy-done.6, bf16[8,256]{1,0:T(8,128)(2,1)S(1)} %copy-done.7, ...), custom_call_target="tpu_custom_call" | custom-call | flops 1207959552 | bytes 9437184 | tf_op jit(solution)/shard_map/pallas_call | solution.py:449
  48.7 0.6 %copy.14 = bf16[8,4096]{1,0:T(8,128)(2,1)} copy(bf16[8,4096]{1,0:T(8,128)(2,1)S(1)} %shard_map.118) | data formatting | bytes 131072
Async XLA Ops:
  0.0 1.9 %copy-start = (bf16[1,4096,384]{2,1,0:T(8,128)(2,1)S(1)}, bf16[1,4096,384]{2,1,0:T(8,128)(2,1)}, u32[]{:S(2)}) copy-start(bf16[1,4096,384]{2,1,0:T(8,128)(2,1)} %gate_hbm.1) | copy-start | bytes 9437188
  1.9 0.9 %copy-start.1 = (bf16[8,32,256]{2,1,0:T(8,128)(2,1)S(1)}, bf16[8,32,256]{2,1,0:T(8,128)(2,1)}, u32[]{:S(2)}) copy-start(bf16[8,32,256]{2,1,0:T(8,128)(2,1)} %keys_ref.1) | copy-start | bytes 393220
  2.8 0.9 %copy-start.2 = (bf16[8,32,256]{2,1,0:T(8,128)(2,1)S(1)}, bf16[8,32,256]{2,1,0:T(8,128)(2,1)}, u32[]{:S(2)}) copy-start(bf16[8,32,256]{2,1,0:T(8,128)(2,1)} %values_ref.1) | copy-start | bytes 393220
  3.7 0.8 %copy-start.3 = (bf16[8,4096]{1,0:T(8,128)(2,1)S(1)}, bf16[8,4096]{1,0:T(8,128)(2,1)}, u32[]{:S(2)}) copy-start(bf16[8,4096]{1,0:T(8,128)(2,1)} %hidden_ref.1) | copy-start | bytes 196612
  4.5 0.8 %copy-start.4 = (bf16[8,4096]{1,0:T(8,128)(2,1)S(1)}, bf16[8,4096]{1,0:T(8,128)(2,1)}, u32[]{:S(2)}) copy-start(bf16[8,4096]{1,0:T(8,128)(2,1)} %query_ref.1) | copy-start | bytes 196612
  5.4 0.7 %copy-start.5 = (f32[4096]{0:T(1024)S(1)}, f32[4096]{0:T(1024)}, u32[]{:S(2)}) copy-start(f32[4096]{0:T(1024)} %param.18) | copy-start | bytes 49156
  6.1 0.7 %copy-start.6 = (bf16[8,256]{1,0:T(8,128)(2,1)S(1)}, bf16[8,256]{1,0:T(8,128)(2,1)}, u32[]{:S(2)}) copy-start(bf16[8,256]{1,0:T(8,128)(2,1)} %new_key_ref.1) | copy-start | bytes 12292
  6.8 0.7 %copy-start.7 = (bf16[8,256]{1,0:T(8,128)(2,1)S(1)}, bf16[8,256]{1,0:T(8,128)(2,1)}, u32[]{:S(2)}) copy-start(bf16[8,256]{1,0:T(8,128)(2,1)} %new_value_ref.1) | copy-start | bytes 12292
  7.5 0.7 %copy-start.8 = (s32[8,8]{1,0:T(8,128)S(1)}, s32[8,8]{1,0:T(8,128)}, u32[]{:S(2)}) copy-start(s32[8,8]{1,0:T(8,128)} %ids_ref.1) | copy-start | bytes 772
  8.2 0.7 %copy-start.9 = (f32[8,8]{1,0:T(8,128)S(1)}, f32[8,8]{1,0:T(8,128)}, u32[]{:S(2)}) copy-start(f32[8,8]{1,0:T(8,128)} %gates_ref.1) | copy-start | bytes 772

commit v2 on v1

--- a/solution.py
+++ b/solution.py
@@ -197,6 +197,19 @@
 
 def layer_kernel(
     chips,
+    hidden_hbm,
+    query_hbm,
+    keys_hbm,
+    values_hbm,
+    new_key_hbm,
+    new_value_hbm,
+    gain_hbm,
+    ids_hbm,
+    gates_hbm,
+    gate_hbm,
+    up_hbm,
+    down_hbm,
+    out_ref,
     hidden_ref,
     query_ref,
     keys_ref,
@@ -206,10 +219,6 @@
     gain_ref,
     ids_ref,
     gates_ref,
-    gate_hbm,
-    up_hbm,
-    down_hbm,
-    out_ref,
     gate,
     up,
     down,
@@ -225,6 +234,7 @@
     replies,
     answers,
     mixed,
+    input_sem,
     weight_sem,
     send_sem,
     recv_sem,
@@ -243,6 +253,23 @@
     my_chip, core = me // 2, me % 2
     sibling = my_chip * 2 + (1 - core)
 
+    staged = (
+        (query_hbm, query_ref),
+        (keys_hbm, keys_ref),
+        (values_hbm, values_ref),
+        (new_key_hbm, new_key_ref),
+        (new_value_hbm, new_value_ref),
+        (hidden_hbm, hidden_ref),
+        (gain_hbm, gain_ref),
+        (ids_hbm, ids_ref),
+        (gates_hbm, gates_ref),
+    )
+    input_copies = [
+        pltpu.make_async_copy(source, target, input_sem.at[i])
+        for i, (source, target) in enumerate(staged)
+    ]
+    for copy in input_copies:
+        copy.start()
     weight_copies = [
         pltpu.make_async_copy(source.at[0], target, weight_sem.at[i])
         for i, (source, target) in enumerate(((gate_hbm, gate), (up_hbm, up), (down_hbm, down)))
@@ -264,6 +291,8 @@
         barrier, inc=1, device_id={"ep": sibling}, device_id_type=pl.DeviceIdType.MESH
     )
 
+    for copy in input_copies:
+        copy.wait()
     normed = attention_rows(
         hidden_ref, query_ref, keys_ref, values_ref, new_key_ref, new_value_ref, gain_ref
     )
@@ -443,15 +472,27 @@
     slots = chips * BLOCK
     units = w_gate.shape[2]
     pair_rows = 2 * chips * CAPACITY
+    small = (
+        hidden,
+        query,
+        cached_key_store,
+        cached_value_store,
+        current_key,
+        current_value,
+        norm_gain.reshape(1, width),
+        expert_ids,
+        gate_weights,
+    )
     dma = pltpu.SemaphoreType.DMA
     vmem = pl.BlockSpec(memory_space=pltpu.VMEM)
-    hbm = pl.BlockSpec(memory_space=pl.ANY)
+    hbm = pl.BlockSpec(memory_space=pltpu.HBM)
     return pl.pallas_call(
         functools.partial(layer_kernel, chips),
         out_shape=jax.ShapeDtypeStruct(hidden.shape, BF16),
-        in_specs=[vmem] * 9 + [hbm] * 3,
+        in_specs=[hbm] * 12,
         out_specs=vmem,
-        scratch_shapes=[
+        scratch_shapes=[pltpu.VMEM(x.shape, x.dtype) for x in small]
+        + [
             pltpu.VMEM((width, units), BF16),
             pltpu.VMEM((width, units), BF16),
             pltpu.VMEM((units, width), BF16),
@@ -467,6 +508,7 @@
             pltpu.VMEM((PARTS, slots, part // 4), BF16),
             pltpu.VMEM((PARTS, slots, part // 4), BF16),
             pltpu.VMEM((4 * ROWS, slots), F32),
+            dma((9,)),
             dma((3,)),
             dma((PARTS, chips)),
             dma((PARTS, chips)),
@@ -478,27 +520,14 @@
             dma((PARTS, chips)),
         ],
         compiler_params=pltpu.CompilerParams(
-            collective_id=0, has_side_effects=True, vmem_limit_bytes=48 * 1024 * 1024
+            collective_id=0, has_side_effects=True, vmem_limit_bytes=62 * 1024 * 1024
         ),
         cost_estimate=pl.CostEstimate(
             flops=6 * pair_rows * width * units,
             bytes_accessed=6 * width * units,
             transcendentals=pair_rows * units,
         ),
-    )(
-        hidden,
-        query,
-        cached_key_store,
-        cached_value_store,
-        current_key,
-        current_value,
-        norm_gain.reshape(1, width),
-        expert_ids,
-        gate_weights,
-        w_gate,
-        w_up,
-        w_down,
-    )
+    )(*small, w_gate, w_up, w_down)
 
 
 def takes_fused_layer(row_count, chosen_count, units):

time: 49.8 us -> 42 us (0.84)
  local copies, waits for them, and re-layouts: 9.47 us -> 1.47 us
  Pallas kernels: 39.8 us -> 40.4 us
    unnamed x21 -> x1, local copies, waits for them, and re-layouts: 9.47 us -> 1.47 us
    pallas_call x1, Pallas kernels: 39.8 us -> 40.4 us  [fused_layer(): pl.pallas_call(functools.partial(layer_kernel, chips), out_shape=jax.Shap...]
where the time goes in v2:
time: 42 us; the launch traced here: 41.8 us
  Pallas kernels  40.4 us (96%)
  local copies, waits for them, and re-layouts  1.47 us (4%)
    pallas_call x1, Pallas kernels, fused_layer(): pl.pallas_call(functools.partial(layer_kernel, chips), out_shape=jax.Shap...  40.4 us
    unnamed x1, local copies, waits for them, and re-layouts  1.47 us

profile of v2, /device:TPU:0, one launch (start us, length us, event | category | flops | bytes accessed | tf_op | source)
XLA Modules:
  0.0 41.8 jit_solution(3450748527663776696)
XLA Ops:
  0.0 40.4 %shard_map.118 = bf16[8,4096]{1,0:T(8,128)(2,1)} custom-call(bf16[8,4096]{1,0:T(8,128)(2,1)} %hidden_hbm.1, bf16[8,4096]{1,0:T(8,128)(2,1)} %query_hbm.1, bf16[8,32,256]{2,1,0:T(8,128)(2,1)} %keys_hbm.1, bf16[8,32,256]{2,1,0:T(8,128)(2,1)} %values_hbm.1, bf16[8,256]{1,0:T(8,128)(2,1)} %new_key_hbm.1, bf16[8,256]{1,0:T(8,128)(2,1)} %new_value_hbm.1, ...), custom_call_target="tpu_custom_call" | custom-call | flops 1207959552 | bytes 9437184 | tf_op jit(solution)/shard_map/pallas_call | solution.py:489
  40.4 1.5 %copy.14 = bf16[8,4096]{1,0:T(8,128)(2,1)} copy(bf16[8,4096]{1,0:T(8,128)(2,1)} %shard_map.118) | data formatting | bytes 131072

commit v3 on v2

--- a/solution.py
+++ b/solution.py
@@ -127,6 +127,7 @@
 ROWS = 8
 BLOCK = 16
 PARTS = 2
+PLANE = 4
 F32 = jnp.float32
 BF16 = jnp.bfloat16
 
@@ -172,27 +173,32 @@
     return resid * lax.rsqrt(meansq + epsilon) * gain_ref[...]
 
 
-def slot_weights(ids_ref, gates_ref, chips, my_chip):
+def slot_weights(routes_ref, chips, my_plane, my_place):
     slots = chips * BLOCK
+    levels = chips // PLANE
     place = lax.broadcasted_iota(jnp.int32, (ROWS, slots), 1)
     token = lax.broadcasted_iota(jnp.int32, (ROWS, slots), 0)
-    expert = (place // BLOCK + my_chip) % chips
+    expert = my_plane * PLANE + (place // (BLOCK * levels) + my_place) % PLANE
+    expert = expert.astype(F32)
+    level = (place // BLOCK) % levels
     quarter = 2 * ((place // 8) % 2) + ((place // 4) % 2 + (place // BLOCK) % 2) % 2
-    chosen = jnp.zeros((ROWS, slots), F32)
-    weight = jnp.zeros((ROWS, slots), F32)
-    for k in range(ids_ref.shape[1]):
-        hit = ids_ref[:, k : k + 1] == expert
-        chosen = jnp.where(hit, 1.0, chosen)
-        weight = jnp.where(hit, gates_ref[:, k : k + 1], weight)
-    rank = jnp.zeros((ROWS, slots), F32)
-    for t in range(ROWS - 1):
-        rank = rank + jnp.where(token > t, chosen[t : t + 1, :], 0.0)
-    live = jnp.where(rank == (place % CAPACITY).astype(F32), chosen, 0.0)
-    picker = jnp.concatenate([jnp.where(quarter == q, live, 0.0) for q in range(4)], axis=0)
-    mixing = jnp.concatenate(
-        [jnp.where(quarter == q, live * weight, 0.0) for q in range(4)], axis=0
-    )
-    return picker, mixing
+    picked, mixed = [], []
+    for j in range(levels):
+        ids, weights = routes_ref[j, 0:ROWS, :], routes_ref[j, ROWS : 2 * ROWS, :]
+        chosen = jnp.zeros((ROWS, slots), F32)
+        weight = jnp.zeros((ROWS, slots), F32)
+        for k in range(ROWS):
+            hit = ids[:, k : k + 1] == expert
+            chosen = jnp.where(hit, 1.0, chosen)
+            weight = jnp.where(hit, weights[:, k : k + 1], weight)
+        rank = jnp.zeros((ROWS, slots), F32)
+        for t in range(ROWS - 1):
+            rank = rank + jnp.where(token > t, chosen[t : t + 1, :], 0.0)
+        live = jnp.where(rank == (place % CAPACITY).astype(F32), chosen, 0.0)
+        live = jnp.where(level == j, live, 0.0)
+        picked += [jnp.where(quarter == q, live, 0.0) for q in range(4)]
+        mixed += [jnp.where(quarter == q, live * weight, 0.0) for q in range(4)]
+    return jnp.concatenate(picked, axis=0), jnp.concatenate(mixed, axis=0)
 
 
 def layer_kernel(
@@ -222,6 +228,8 @@
     gate,
     up,
     down,
+    routes,
+    line_rows,
     outgoing,
     arrived,
     row_buffer,
@@ -234,8 +242,17 @@
     replies,
     answers,
     mixed,
+    sums_out,
+    sums_in,
+    own_sums,
     input_sem,
     weight_sem,
+    route_send,
+    route_recv,
+    line_send,
+    line_recv,
+    sum_send,
+    sum_recv,
     send_sem,
     recv_sem,
     pass_send,
@@ -249,8 +266,12 @@
     part = width // PARTS
     quarter = part // 4
     plane_rows = chips * CAPACITY
+    levels = chips // PLANE
+    group_rows = levels * BLOCK
+    line = 4 * ROWS
     me = lax.axis_index("ep")
     my_chip, core = me // 2, me % 2
+    my_plane, my_place = my_chip // PLANE, my_chip % PLANE
     sibling = my_chip * 2 + (1 - core)
 
     staged = (
@@ -277,51 +298,102 @@
     for copy in weight_copies:
         copy.start()
 
-    def peer(offset):
-        return {"ep": ((my_chip + offset) % chips) * 2 + core}
+    def beside(offset):
+        return {"ep": (my_plane * PLANE + (my_place + offset) % PLANE) * 2 + core}
+
+    def along(offset):
+        return {"ep": (((my_plane + offset) % levels) * PLANE + my_place) * 2 + core}
 
     barrier = pltpu.get_barrier_semaphore()
-
-    def greet(k, carry):
-        pl.semaphore_signal(barrier, inc=1, device_id=peer(k), device_id_type=pl.DeviceIdType.MESH)
-        return carry
-
-    lax.fori_loop(1, chips, greet, 0)
-    pl.semaphore_signal(
-        barrier, inc=1, device_id={"ep": sibling}, device_id_type=pl.DeviceIdType.MESH
-    )
+    mesh_ids = pl.DeviceIdType.MESH
+    for j in range(1, levels):
+        pl.semaphore_signal(barrier, inc=1, device_id=along(j), device_id_type=mesh_ids)
+    for k in range(1, PLANE):
+        pl.semaphore_signal(barrier, inc=1, device_id=beside(k), device_id_type=mesh_ids)
+    pl.semaphore_signal(barrier, inc=1, device_id={"ep": sibling}, device_id_type=mesh_ids)
+
+    def send(source, target, send_flag, recv_flag, device):
+        return pltpu.make_async_remote_copy(
+            src_ref=source,
+            dst_ref=target,
+            send_sem=send_flag,
+            recv_sem=recv_flag,
+            device_id=device,
+            device_id_type=mesh_ids,
+        )
+
+    def group(k):
+        return slice(k * group_rows, (k + 1) * group_rows)
+
+    def lines(j):
+        return slice(j * line, (j + 1) * line)
+
+    def route(j):
+        return send(routes.at[0], routes.at[j], route_send.at[j], route_recv.at[j], along(j))
+
+    def spread_row(h, j):
+        return send(
+            line_rows.at[h, lines(0)],
+            line_rows.at[h, lines(j)],
+            line_send.at[h, j],
+            line_recv.at[h, j],
+            along(j),
+        )
+
+    def dispatch(h, k):
+        return send(
+            outgoing.at[h, group(k)],
+            arrived.at[h, 0, group(k)],
+            send_sem.at[h, k],
+            recv_sem.at[h, k],
+            beside(k),
+        )
+
+    def pass_on(h, k):
+        return send(
+            arrived.at[h, 0, group(k)],
+            arrived.at[h, 1, group(k)],
+            pass_send.at[h, k],
+            pass_recv.at[h, k],
+            {"ep": sibling},
+        )
+
+    def reply(h, k):
+        return send(
+            replies.at[h, group(k)],
+            answers.at[h, group(k)],
+            reply_send.at[h, k],
+            reply_recv.at[h, k],
+            beside(PLANE - k),
+        )
+
+    def send_sum(h, j):
+        return send(
+            sums_out.at[h, lines(j)],
+            sums_in.at[h, lines(j)],
+            sum_send.at[h, j],
+            sum_recv.at[h, j],
+            along(levels - j),
+        )
 
     for copy in input_copies:
         copy.wait()
+    routes[0] = jnp.zeros(routes.shape[1:], F32)
+    routes[0, 0:ROWS, 0 : ids_ref.shape[1]] = ids_ref[...].astype(F32)
+    routes[0, ROWS : 2 * ROWS, 0 : gates_ref.shape[1]] = gates_ref[...]
     normed = attention_rows(
         hidden_ref, query_ref, keys_ref, values_ref, new_key_ref, new_value_ref, gain_ref
     )
-    picker, mixing = slot_weights(ids_ref, gates_ref, chips, my_chip)
-    picker = picker.T.astype(BF16)
-    mixed[...] = mixing
-
-    def block(k):
-        return pl.ds(pl.multiple_of(k * BLOCK, BLOCK), BLOCK)
-
-    def dispatch(h, k):
-        return pltpu.make_async_remote_copy(
-            src_ref=outgoing.at[h, block(k)],
-            dst_ref=arrived.at[h, 0, block(k)],
-            send_sem=send_sem.at[h, k],
-            recv_sem=recv_sem.at[h, k],
-            device_id=peer(k),
-            device_id_type=pl.DeviceIdType.MESH,
-        )
-
-    def pass_on(h, k):
-        return pltpu.make_async_remote_copy(
-            src_ref=arrived.at[h, 0, block(k)],
-            dst_ref=arrived.at[h, 1, block(k)],
-            send_sem=pass_send.at[h, k],
-            recv_sem=pass_recv.at[h, k],
-            device_id={"ep": sibling},
-            device_id_type=pl.DeviceIdType.MESH,
-        )
+    for h in range(PARTS):
+        line_rows[h, lines(0)] = jnp.concatenate(
+            [normed[:, h * part + q * quarter : h * part + (q + 1) * quarter] for q in range(4)],
+            axis=0,
+        ).astype(BF16)
+    pl.semaphore_wait(barrier, levels + PLANE - 1)
+    for j in range(1, levels):
+        route(j).start()
+    for j in range(1, levels):
+        spread_row(0, j).start()
 
     def swap(h):
         return pltpu.make_async_remote_copy(
@@ -333,51 +405,43 @@
             device_id_type=pl.DeviceIdType.MESH,
         )
 
-    def reply(h, k):
-        return pltpu.make_async_remote_copy(
-            src_ref=replies.at[h, block(k)],
-            dst_ref=answers.at[h, block(k)],
-            send_sem=reply_send.at[h, k],
-            recv_sem=reply_recv.at[h, k],
-            device_id=peer(chips - k),
-            device_id_type=pl.DeviceIdType.MESH,
-        )
-
-    def each(first, body):
-        def step(k, carry):
-            body(k)
-            return carry
-
-        lax.fori_loop(first, chips, step, 0)
-
-    for h in range(PARTS):
-        stacked = jnp.concatenate(
-            [normed[:, h * part + q * quarter : h * part + (q + 1) * quarter] for q in range(4)],
-            axis=0,
-        ).astype(BF16)
-        packed = jnp.dot(picker, stacked, preferred_element_type=F32).astype(BF16)
+    for j in range(1, levels):
+        route(j).wait_recv()
+    picker, mixing = slot_weights(routes, chips, my_plane, my_place)
+    picker = picker.T.astype(BF16)
+    mixed[...] = mixing
+
+    def pack(h):
+        for j in range(1, levels):
+            spread_row(h, j).wait_send()
+        if h + 1 < PARTS:
+            for j in range(1, levels):
+                spread_row(h + 1, j).start()
+        for j in range(1, levels):
+            spread_row(h, j).wait_recv()
+        packed = jnp.dot(picker, line_rows[h], preferred_element_type=F32).astype(BF16)
         outgoing[h] = packed
-        arrived[h, 0, 0:BLOCK] = packed[0:BLOCK]
-        if h == 0:
-            pl.semaphore_wait(barrier, chips)
-        each(1, lambda k: dispatch(h, k).start())
+        arrived[h, 0, group(0)] = packed[group(0)]
+        for k in range(1, PLANE):
+            dispatch(h, k).start()
         pass_on(h, 0).start()
 
+    pack(0)
     low = lax.broadcasted_iota(jnp.int32, (chips // 2, 8, quarter), 1) < 4
 
     def swap_halves(x):
         return pltpu.roll(x, 4, axis=1)
 
     for h in range(PARTS):
-
-        def relay(k):
+        if h + 1 < PARTS:
+            pack(h + 1)
+        for k in range(1, PLANE):
             dispatch(h, k).wait_recv()
             pass_on(h, k).start()
-
-        each(1, relay)
         for plane in range(2):
             if plane == 1:
-                each(0, lambda k: pass_on(h, k).wait_recv())
+                for k in range(PLANE):
+                    pass_on(h, k).wait_recv()
             tiles = arrived[h, plane].astype(F32).reshape(chips // 2, 2, 2, 8, quarter)
             for p in range(2):
                 a, b = tiles[:, 0, p], tiles[:, 1, p]
@@ -410,6 +474,24 @@
             mine[:, columns] = y[:plane_rows]
             give[h, :, q * quarter : (q + 1) * quarter] = y[plane_rows:].astype(BF16)
         swap(h).start()
+    mixing = mixed[...]
+    high = mixing.astype(BF16)
+    rest = mixing - high.astype(F32)
+    middle = rest.astype(BF16)
+    last = (rest - middle.astype(F32)).astype(BF16)
+
+    def combine(h):
+        for k in range(1, PLANE):
+            reply(h, k).wait_recv()
+        got = answers[h]
+        total = jnp.dot(high, got, preferred_element_type=F32)
+        total = total + jnp.dot(middle, got, preferred_element_type=F32)
+        total = total + jnp.dot(last, got, preferred_element_type=F32)
+        own_sums[h] = total[lines(0)]
+        sums_out[h] = total.astype(BF16)
+        for j in range(1, levels):
+            send_sum(h, j).start()
+
     for h in range(PARTS):
         swap(h).wait_recv()
         halves = []
@@ -427,29 +509,37 @@
                 replies[h, start : start + BLOCK] = jnp.concatenate(
                     [halves[0][side][m], halves[1][side][m]], axis=0
                 ).astype(BF16)
-        answers[h, 0:BLOCK] = replies[h, 0:BLOCK]
-        each(1, lambda k: reply(h, k).start())
-
-    mixing = mixed[...]
-    high = mixing.astype(BF16)
-    rest = mixing - high.astype(F32)
-    middle = rest.astype(BF16)
-    last = (rest - middle.astype(F32)).astype(BF16)
+        answers[h, group(0)] = replies[h, group(0)]
+        if h > 0:
+            for k in range(1, PLANE):
+                reply(h - 1, k).wait_send()
+        for k in range(1, PLANE):
+            reply(h, k).start()
+        if h > 0:
+            combine(h - 1)
+
+    combine(PARTS - 1)
     for h in range(PARTS):
-        each(1, lambda k: reply(h, k).wait_recv())
-        got = answers[h]
-        total = jnp.dot(high, got, preferred_element_type=F32)
-        total = total + jnp.dot(middle, got, preferred_element_type=F32)
-        total = total + jnp.dot(last, got, preferred_element_type=F32)
+        total = own_sums[h]
+        for j in range(1, levels):
+            send_sum(h, j).wait_recv()
+            total = total + sums_in[h, lines(j)].astype(F32)
         for q in range(4):
             columns = slice(h * part + q * quarter, h * part + (q + 1) * quarter)
             out_ref[:, columns] = total[q * ROWS : (q + 1) * ROWS].astype(out_ref.dtype)
 
+    for j in range(1, levels):
+        route(j).wait_send()
+    for k in range(1, PLANE):
+        reply(PARTS - 1, k).wait_send()
     for h in range(PARTS):
-        each(1, lambda k: dispatch(h, k).wait_send())
-        each(0, lambda k: pass_on(h, k).wait_send())
+        for j in range(1, levels):
+            send_sum(h, j).wait_send()
+        for k in range(1, PLANE):
+            dispatch(h, k).wait_send()
+        for k in range(PLANE):
+            pass_on(h, k).wait_send()
         swap(h).wait_send()
-        each(1, lambda k: reply(h, k).wait_send())
 
 
 def fused_layer(
@@ -472,6 +562,8 @@
     slots = chips * BLOCK
     units = w_gate.shape[2]
     pair_rows = 2 * chips * CAPACITY
+    levels = chips // PLANE
+    line_rows = levels * 4 * ROWS
     small = (
         hidden,
         query,
@@ -496,6 +588,8 @@
             pltpu.VMEM((width, units), BF16),
             pltpu.VMEM((width, units), BF16),
             pltpu.VMEM((units, width), BF16),
+            pltpu.VMEM((levels, 2 * ROWS, 128), F32),
+            pltpu.VMEM((PARTS, line_rows, part // 4), BF16),
             pltpu.VMEM((PARTS, slots, part // 4), BF16),
             pltpu.VMEM((PARTS, 2, slots, part // 4), BF16),
             pltpu.VMEM((pair_rows, width), BF16),
@@ -507,17 +601,26 @@
             pltpu.VMEM((PARTS, pair_rows // 2, part), BF16),
             pltpu.VMEM((PARTS, slots, part // 4), BF16),
             pltpu.VMEM((PARTS, slots, part // 4), BF16),
-            pltpu.VMEM((4 * ROWS, slots), F32),
+            pltpu.VMEM((line_rows, slots), F32),
+            pltpu.VMEM((PARTS, line_rows, part // 4), BF16),
+            pltpu.VMEM((PARTS, line_rows, part // 4), BF16),
+            pltpu.VMEM((PARTS, 4 * ROWS, part // 4), F32),
             dma((9,)),
             dma((3,)),
-            dma((PARTS, chips)),
-            dma((PARTS, chips)),
-            dma((PARTS, chips)),
-            dma((PARTS, chips)),
+            dma((levels,)),
+            dma((levels,)),
+            dma((PARTS, levels)),
+            dma((PARTS, levels)),
+            dma((PARTS, levels)),
+            dma((PARTS, levels)),
+            dma((PARTS, PLANE)),
+            dma((PARTS, PLANE)),
+            dma((PARTS, PLANE)),
+            dma((PARTS, PLANE)),
             dma((PARTS,)),
             dma((PARTS,)),
-            dma((PARTS, chips)),
-            dma((PARTS, chips)),
+            dma((PARTS, PLANE)),
+            dma((PARTS, PLANE)),
         ],
         compiler_params=pltpu.CompilerParams(
             collective_id=0, has_side_effects=True, vmem_limit_bytes=62 * 1024 * 1024
@@ -534,7 +637,9 @@
     if lax.axis_size("sub") != 1 or lax.axis_size("group") != 1 or 2 * units != FF:
         return False
     chips = lax.axis_size("ep") // 2
-    return row_count == ROWS and chips * CAPACITY == row_count * chosen_count and chips % 2 == 0
+    if row_count != ROWS or chosen_count != ROWS or chips % PLANE != 0:
+        return False
+    return chips * CAPACITY == row_count * chosen_count
 
 
 def shards(

time: 42 us -> 39.4 us (0.938)
  Pallas kernels: 40.4 us -> 37.7 us
    pallas_call x1, Pallas kernels: 40.4 us -> 37.7 us  [fused_layer(): pl.pallas_call(functools.partial(layer_kernel, chips), out_shape=jax.Shap...]
where the time goes in v3:
time: 39.4 us; the launch traced here: 39.2 us
  Pallas kernels  37.7 us (96%)
  local copies, waits for them, and re-layouts  1.47 us (4%)
    pallas_call x1, Pallas kernels, fused_layer(): pl.pallas_call(functools.partial(layer_kernel, chips), out_shape=jax.Shap...  37.7 us
    unnamed x1, local copies, waits for them, and re-layouts  1.47 us

profile of v3, /device:TPU:0, one launch (start us, length us, event | category | flops | bytes accessed | tf_op | source)
XLA Modules:
  0.0 39.2 jit_solution(13097728814015585769)
XLA Ops:
  0.0 37.7 %shard_map.118 = bf16[8,4096]{1,0:T(8,128)(2,1)} custom-call(bf16[8,4096]{1,0:T(8,128)(2,1)} %hidden_hbm.1, bf16[8,4096]{1,0:T(8,128)(2,1)} %query_hbm.1, bf16[8,32,256]{2,1,0:T(8,128)(2,1)} %keys_hbm.1, bf16[8,32,256]{2,1,0:T(8,128)(2,1)} %values_hbm.1, bf16[8,256]{1,0:T(8,128)(2,1)} %new_key_hbm.1, bf16[8,256]{1,0:T(8,128)(2,1)} %new_value_hbm.1, ...), custom_call_target="tpu_custom_call" | custom-call | flops 1207959552 | bytes 9437184 | tf_op jit(solution)/shard_map/pallas_call | solution.py:581
  37.8 1.5 %copy.14 = bf16[8,4096]{1,0:T(8,128)(2,1)} copy(bf16[8,4096]{1,0:T(8,128)(2,1)} %shard_map.118) | data formatting | bytes 131072
